TPU v7x, 1024 devices: a whole 8x8x8 slice. The times are simulated.
1024 devices in a mesh: gx: 8 (over y_hi, core), gy: 8 (over z), gz: 16 (over y_lo, x).
Axes of the slice: x: 8, y: 8 (y_hi: 4, y_lo: 2; y = y_hi * 2 + y_lo), z: 8, core: 2. Of those that a mesh axis runs over, the one named last changes fastest.
Arguments:
- conc: float32 [2, 128, 256, 1024], P(None, 'gz', 'gx', 'gy'), may hold values from -4 to 4
- speed: float32 [3, 128, 256, 1024], P(None, 'gz', 'gx', 'gy'), may hold values from 0.02 to 0.15
- rates: float32 [2, 128, 256, 1024], P(None, 'gz', 'gx', 'gy'), may hold values from 0.005 to 0.06
- region: int32 [128, 256, 1024], P('gz', 'gx', 'gy'), may hold values 0 or 1
- flow_signs: int32 [16, 8, 8], P('gz', 'gx', 'gy'), may hold values from 0 to 7
Outputs:
- final: float32 [2, 128, 256, 1024], P(None, 'gz', 'gx', 'gy')
Inputs may be any that keep to these rules, and one draw needn't show every extreme that they name: `flow_signs`: bit 0, 1, 2 set: flow toward lower z, x, y in that subdomain.
All inputs are finite; a program needn't handle non-finite values. No bound on the sum of `region` on one device may be relied on, other than what follows from the above.
Results may differ from a plain program's by a relative error of at most 0.000088.
Values sent between devices are 32-bit elements; how exact they have to be, the bound alone decides.
A program may use at most 32 MiB of HBM per device.

v0:
```python
import jax
import jax.numpy as jnp
from jax import lax
from jax.sharding import PartitionSpec as P

NT = 16
ITERS = 3


ROBIN = 0.5
DIFFUSE = 0.07


def extended(array, sides, width):
    for axis, dim in sides:
        peers, length = (lax.axis_size(axis), array.shape[dim])
        up = [(i, (i + 1) % peers) for i in range(peers)]
        down = [(j, i) for i, j in up]
        last = lax.slice_in_dim(array, length - width, length, axis=dim)
        initial = lax.slice_in_dim(array, 0, width, axis=dim)
        before = lax.ppermute(last, axis, up)
        after = lax.ppermute(initial, axis, down)
        array = jnp.concatenate([before, array, after], axis=dim)
    return array


def layer(field, along, index):
    return lax.index_in_dim(field, index, axis=along, keepdims=False)


def advance(field, ghosts, speeds, rate, region_f, against):

    def neighbours(lower, upper, along):
        padded = jnp.concatenate(
            [jnp.expand_dims(lower, along), field, jnp.expand_dims(upper, along)], axis=along
        )
        extent = field.shape[along]
        return (
            lax.slice_in_dim(padded, 0, extent, axis=along),
            lax.slice_in_dim(padded, 2, extent + 2, axis=along),
        )

    lower_z, upper_z = neighbours(ghosts[0], ghosts[1], 1)
    lower_x, upper_x = neighbours(ghosts[2], ghosts[3], 2)
    lower_y, upper_y = neighbours(ghosts[4], ghosts[5], 3)
    total = lower_z + upper_z + (lower_x + upper_x) + (lower_y + upper_y)
    spread = DIFFUSE * (total - 6.0 * field)
    carry_z = speeds[0] * jnp.where(against[0], field - upper_z, field - lower_z)
    carry_x = speeds[1] * jnp.where(against[1], field - upper_x, field - lower_x)
    carry_y = speeds[2] * jnp.where(against[2], field - upper_y, field - lower_y)
    carried = carry_z + carry_x + carry_y
    change = region_f * (rate[1] * field[1] - rate[0] * field[0])
    reaction = jnp.stack([change, -change])
    return field + (spread - carried + reaction)


def face_layer(field, along, index):
    picked = layer(field, along, index)
    if along == 3:
        return picked.reshape(picked.shape[0], -1)
    return picked


def outer_layers(field, along):
    extent = field.shape[along]
    return jnp.stack(
        [
            face_layer(field, along, 0),
            face_layer(field, along, 1),
            face_layer(field, along, extent - 2),
            face_layer(field, along, extent - 1),
        ],
        axis=0,
    )


def pack(field):
    z_side = outer_layers(field, 1)
    x_side = outer_layers(field, 2)
    y_side = outer_layers(field, 3)
    return (z_side, x_side, y_side)


def trade(packs):
    width = 2
    z_recv = extended(packs[0], (("gz", 1),), width)
    x_recv = extended(packs[1], (("gx", 1),), width)
    y_recv = extended(packs[2], (("gy", 1),), width)
    return (z_recv, x_recv, y_recv)


def decode(received, y_shape):
    result = []
    for which, arrived in enumerate(received):
        lower = arrived[:, 0] + (ROBIN - 1.0) * arrived[:, 1]
        upper = arrived[:, -1] + (ROBIN - 1.0) * arrived[:, -2]
        if which == 2:
            lower = lower.reshape((lower.shape[0],) + y_shape)
            upper = upper.reshape((upper.shape[0],) + y_shape)
        result.append(lower)
        result.append(upper)
    return tuple(result)


def body(conc, speed, rates, region, flow_signs):
    flags = flow_signs[0, 0, 0]
    against = (flags % 2 == 1, flags // 2 % 2 == 1, flags // 4 % 2 == 1)
    region_f = region.astype(jnp.float32)
    y_shape = (conc.shape[0], conc.shape[1], conc.shape[2])

    def update(field, incoming):
        faces = []
        for along in (1, 2, 3):
            faces.append(layer(field, along, 0))
            faces.append(layer(field, along, field.shape[along] - 1))
        if incoming is None:
            ghosts = tuple(faces)
        else:
            ghosts = tuple(((datum + face) / (1.0 + ROBIN) for datum, face in zip(incoming, faces)))
        return advance(field, ghosts, speed, rates, region_f, against)

    incoming = None
    final_field = conc
    for sweep in range(ITERS):
        sending = sweep + 1 < ITERS

        def stepper(field, ghost_data):
            emitted = pack(field) if sending else ()
            return (update(field, ghost_data), emitted)

        integrate_final_field, stacked = lax.scan(stepper, conc, incoming, length=NT)
        outgoing = decode(trade(stacked), y_shape) if sending else ()
        final_field, outgoing = (integrate_final_field, outgoing)
        incoming = outgoing
    return final_field


def solution(mesh):
    placed = (
        P(None, "gz", "gx", "gy"),
        P(None, "gz", "gx", "gy"),
        P(None, "gz", "gx", "gy"),
        P("gz", "gx", "gy"),
        P("gz", "gx", "gy"),
    )
    return jax.shard_map(
        body, mesh=mesh, in_specs=placed, out_specs=P(None, "gz", "gx", "gy"), check_vma=False
    )
```

profile of v0, /device:TPU:17, one launch (start us, length us, event | category | flops | bytes accessed | tf_op | source)
XLA Modules:
  0.0 704.6 jit_solution(3359390971925498355)
XLA Ops:
  4.4 174.8 %while.42 = (s32[]{:T(128)}, f32[2,8,32,128]{3,2,1,0:T(8,128)S(1)}, f32[16,4,2,32,128]{4,2,3,0,1:T(2,128)S(1)}, f32[16,4,2,8,128]{4,3,2,0,1:T(8,128)}, f32[16,4,...) while((s32[]{:T(128)}, f32[2,8,32,128]{3,2,1,0:T(8,128)S(1)}, ...), condition=%wide.region_1.2_spmd, body=%wide.region_0.1_spmd.sunk | while | flops 2390018 | bytes 6907004 | solution.py:131
  180.7 4.4 collective-permute-start.1
  185.1 1.9 collective-permute-start
  187.7 4.9 collective-permute-start.4
  193.5 3.1 collective-permute-start.3
  196.6 4.3 collective-permute-start.2
  207.1 13.8 %collective-permute-start.5 = (f32[16,2,2,256]{3,2,1,0:T(2,128)}, f32[16,2,2,256]{3,2,1,0:T(2,128)S(1)}, u32[]{:S(2)}, u32[]{:S(2)}) collective-permute-start(f32[16,2,2,256]{3,2,1,0:T(2,128)} %get-tuple-element.534), channel_id=1, source_target_pairs={{16,0},{32,16},{48,32},{64,48},{80,64},{96,80},{112,96},{0,112},{1... | collective-permute-start | bytes 196616 | tf_op jit(solution)/shard_map/ppermute | solution.py:22
  227.3 2.3 fusion.70
  229.7 2.3 fusion.72
  232.0 2.4 broadcast.102.clone.1
  235.9 358.3 %while.43 = (s32[]{:T(128)}, f32[2,8,32,128]{2,1,0,3:T(8,128)S(1)}, f32[16,4,2,32,128]{4,2,3,0,1:T(2,128)}, f32[16,4,2,8,128]{4,3,2,0,1:T(8,128)}, f32[16,4,2,25...) while((s32[]{:T(128)}, f32[2,8,32,128]{2,1,0,3:T(8,128)S(1)}, ...), condition=%wide.region_3.4_spmd, body=%wide.region_2.3_spmd.sunk | while | flops 2433026 | bytes 10098524 | solution.py:131
  250.0 1.9 copy.286
  272.4 1.9 copy.286
  294.8 1.9 copy.286
  317.2 1.9 copy.286
  339.6 1.9 copy.286
  362.0 1.9 copy.286
  384.4 1.9 copy.286
  406.8 1.9 copy.286
  429.2 1.9 copy.286
  451.6 1.9 copy.286
  474.0 1.9 copy.286
  594.2 3.2 fusion.90
  597.4 5.7 collective-permute-start.7
  603.2 1.9 collective-permute-start.6
  605.1 1.9 collective-permute-start.10
  607.9 4.4 collective-permute-start.9
  612.3 2.0 collective-permute-start.8
  614.4 5.7 collective-permute-done.10
  620.0 7.5 %collective-permute-start.11 = (f32[16,2,2,256]{3,2,1,0:T(2,128)S(1)}, f32[16,2,2,256]{3,2,1,0:T(2,128)S(1)}, u32[]{:S(2)}, u32[]{:S(2)}) collective-permute-start(f32[16,2,2,256]{3,2,1,0:T(2,128)S(1)} %get-tuple-element.532), channel_id=1, source_target_pairs={{16,0},{32,16},{48,32},{64,48},{80,64},{96,80},{112,96},{0,112},{1... | collective-permute-start | bytes 196616 | tf_op jit(solution)/shard_map/ppermute | solution.py:22
  630.3 9.9 %collective-permute-done.9 = f32[16,2,2,8,128]{4,3,2,0,1:T(8,128)} collective-permute-done((f32[16,2,2,8,128]{4,3,2,0,1:T(8,128)}, f32[16,2,2,8,128]{4,3,2,0,1:T(8,128)}, u32[]{:S(2)}, u32[]{:S(2)}) %collective-permute-start.9) | collective-permute-done | bytes 262176 | tf_op jit(solution)/shard_map/ppermute | solution.py:22
  643.3 60.4 %while.44 = (s32[]{:T(128)}, f32[2,8,32,128]{3,1,0,2:T(8,128)S(1)}, f32[16,2,32,128]{3,1,2,0:T(2,128)S(1)}, f32[16,2,32,128]{3,1,2,0:T(2,128)}, f32[16,2,8,128]{...) while((s32[]{:T(128)}, f32[2,8,32,128]{3,1,0,2:T(8,128)S(1)}, ...), condition=%wide.region_5.6_spmd, body=%wide.region_4.5_spmd.sunk | while | flops 2304002 | bytes 4415644 | solution.py:131
  (1227 shorter events, 597.4 us)
Async XLA Ops:
  0.0 4.4 copy-start.6
  0.0 4.4 copy-start
  0.0 4.4 copy-start.2
  1.8 199.2 %copy-start.7 = (f32[8,32,128]{2,0,1:T(8,128)}, f32[8,32,128]{2,0,1:T(8,128)S(1)}, u32[]{:S(2)}) copy-start(f32[8,32,128]{2,0,1:T(8,128)S(1)} %copy_convert_fusion) | copy-start | bytes 393220
  179.2 7.9 %copy-start.18 = (f32[16,4,2,256]{3,2,1,0:T(2,128)S(1)}, f32[16,4,2,256]{3,2,1,0:T(2,128)}, u32[]{:S(2)}) copy-start(f32[16,4,2,256]{3,2,1,0:T(2,128)} %get-tuple-element.227) | copy-start | bytes 393220
  179.2 13.5 %copy-start.12 = (f32[16,4,2,8,128]{4,3,2,0,1:T(8,128)S(1)}, f32[16,4,2,8,128]{4,3,2,0,1:T(8,128)}, u32[]{:S(2)}) copy-start(f32[16,4,2,8,128]{4,3,2,0,1:T(8,128)} %get-tuple-element.226) | copy-start | bytes 1572868
  180.7 21.9 %copy-start.5 = (f32[2,8,32,128]{3,2,1,0:T(8,128)S(1)}, f32[2,8,32,128]{3,2,1,0:T(8,128)}, u32[]{:S(2)}) copy-start(f32[2,8,32,128]{3,2,1,0:T(8,128)} %param.11) | copy-start | bytes 786436
  180.7 46.7 %collective-permute-start.1 = (f32[16,2,2,32,128]{4,2,3,0,1:T(2,128)}, f32[16,2,2,32,128]{4,2,3,0,1:T(2,128)}, u32[]{:S(2)}, u32[]{:S(2)}) collective-permute-start(f32[16,2,2,32,128]{4,2,3,0,1:T(2,128)} %get-tuple-element.526), channel_id=1, source_target_pairs={{1,0},{2,1},{3,2},{4,3},{5,4},{6,5},{7,6},{8,7},{9,8},{10,9},{11,1... | collective-permute-start | bytes 3145736 | tf_op jit(solution)/shard_map/ppermute | solution.py:22
  185.1 44.6 %collective-permute-start = (f32[16,2,2,32,128]{4,2,3,0,1:T(2,128)}, f32[16,2,2,32,128]{4,2,3,0,1:T(2,128)}, u32[]{:S(2)}, u32[]{:S(2)}) collective-permute-start(f32[16,2,2,32,128]{4,2,3,0,1:T(2,128)} %get-tuple-element.527), channel_id=1, source_target_pairs={{0,1},{1,2},{2,3},{3,4},{4,5},{5,6},{6,7},{7,8},{8,9},{9,10},{10,1... | collective-permute-start | bytes 3145736 | tf_op jit(solution)/shard_map/ppermute | solution.py:21
  187.7 19.4 %collective-permute-start.4 = (f32[16,2,2,256]{3,2,1,0:T(2,128)}, f32[16,2,2,256]{3,2,1,0:T(2,128)}, u32[]{:S(2)}, u32[]{:S(2)}) collective-permute-start(f32[16,2,2,256]{3,2,1,0:T(2,128)} %get-tuple-element.535), channel_id=1, source_target_pairs={{0,16},{16,32},{32,48},{48,64},{64,80},{80,96},{96,112},{112,0},{1... | collective-permute-start | bytes 196616 | tf_op jit(solution)/shard_map/ppermute | solution.py:21
  193.5 30.6 %collective-permute-start.3 = (f32[16,2,2,8,128]{4,3,2,0,1:T(8,128)}, f32[16,2,2,8,128]{4,3,2,0,1:T(8,128)}, u32[]{:S(2)}, u32[]{:S(2)}) collective-permute-start(f32[16,2,2,8,128]{4,3,2,0,1:T(8,128)} %get-tuple-element.530), channel_id=1, source_target_pairs={{128,0},{256,128},{384,256},{512,384},{640,512},{768,640},{896,768... | collective-permute-start | bytes 786440 | tf_op jit(solution)/shard_map/ppermute | solution.py:22
  196.6 29.1 %collective-permute-start.2 = (f32[16,2,2,8,128]{4,3,2,0,1:T(8,128)}, f32[16,2,2,8,128]{4,3,2,0,1:T(8,128)}, u32[]{:S(2)}, u32[]{:S(2)}) collective-permute-start(f32[16,2,2,8,128]{4,3,2,0,1:T(8,128)} %get-tuple-element.531), channel_id=1, source_target_pairs={{0,128},{128,256},{256,384},{384,512},{512,640},{640,768},{768,896... | collective-permute-start | bytes 786440 | tf_op jit(solution)/shard_map/ppermute | solution.py:21
  207.1 15.4 %collective-permute-start.5 = (f32[16,2,2,256]{3,2,1,0:T(2,128)}, f32[16,2,2,256]{3,2,1,0:T(2,128)S(1)}, u32[]{:S(2)}, u32[]{:S(2)}) collective-permute-start(f32[16,2,2,256]{3,2,1,0:T(2,128)} %get-tuple-element.534), channel_id=1, source_target_pairs={{16,0},{32,16},{48,32},{64,48},{80,64},{96,80},{112,96},{0,112},{1... | collective-permute-start | bytes 196616 | tf_op jit(solution)/shard_map/ppermute | solution.py:22
  321.7 3.2 copy-start.15
  344.1 3.2 copy-start.15
  344.1 3.2 copy-start.16
  366.5 3.2 copy-start.15
  366.5 3.2 copy-start.16
  523.3 3.2 copy-start.15
  545.7 3.2 copy-start.15
  594.2 10.9 %copy-start.17 = (f32[16,4,2,256]{3,2,1,0:T(2,128)S(1)}, f32[16,4,2,256]{3,2,1,0:T(2,128)}, u32[]{:S(2)}) copy-start(f32[16,4,2,256]{3,2,1,0:T(2,128)} %get-tuple-element.230) | copy-start | bytes 393220
  594.2 12.8 %copy-start.11 = (f32[16,4,2,8,128]{4,3,2,0,1:T(8,128)S(1)}, f32[16,4,2,8,128]{4,3,2,0,1:T(8,128)}, u32[]{:S(2)}) copy-start(f32[16,4,2,8,128]{4,3,2,0,1:T(8,128)} %get-tuple-element.229) | copy-start | bytes 1572868
  597.4 44.4 %collective-permute-start.7 = (f32[16,2,2,32,128]{4,2,3,0,1:T(2,128)}, f32[16,2,2,32,128]{4,2,3,0,1:T(2,128)S(1)}, u32[]{:S(2)}, u32[]{:S(2)}) collective-permute-start(f32[16,2,2,32,128]{4,2,3,0,1:T(2,128)} %get-tuple-element.524), channel_id=1, source_target_pairs={{1,0},{2,1},{3,2},{4,3},{5,4},{6,5},{7,6},{8,7},{9,8},{10,9},{11,1... | collective-permute-start | bytes 3145736 | tf_op jit(solution)/shard_map/ppermute | solution.py:22
  603.2 39.8 %collective-permute-start.6 = (f32[16,2,2,32,128]{4,2,3,0,1:T(2,128)}, f32[16,2,2,32,128]{4,2,3,0,1:T(2,128)S(1)}, u32[]{:S(2)}, u32[]{:S(2)}) collective-permute-start(f32[16,2,2,32,128]{4,2,3,0,1:T(2,128)} %get-tuple-element.525), channel_id=1, source_target_pairs={{0,1},{1,2},{2,3},{3,4},{4,5},{5,6},{6,7},{7,8},{8,9},{9,10},{10,1... | collective-permute-start | bytes 3145736 | tf_op jit(solution)/shard_map/ppermute | solution.py:21
  605.1 14.9 %collective-permute-start.10 = (f32[16,2,2,256]{3,2,1,0:T(2,128)S(1)}, f32[16,2,2,256]{3,2,1,0:T(2,128)S(1)}, u32[]{:S(2)}, u32[]{:S(2)}) collective-permute-start(f32[16,2,2,256]{3,2,1,0:T(2,128)S(1)} %get-tuple-element.533), channel_id=1, source_target_pairs={{0,16},{16,32},{32,48},{48,64},{64,80},{80,96},{96,112},{112,0},{1... | collective-permute-start | bytes 196616 | tf_op jit(solution)/shard_map/ppermute | solution.py:21
  607.9 32.2 %collective-permute-start.9 = (f32[16,2,2,8,128]{4,3,2,0,1:T(8,128)}, f32[16,2,2,8,128]{4,3,2,0,1:T(8,128)}, u32[]{:S(2)}, u32[]{:S(2)}) collective-permute-start(f32[16,2,2,8,128]{4,3,2,0,1:T(8,128)} %get-tuple-element.528), channel_id=1, source_target_pairs={{128,0},{256,128},{384,256},{512,384},{640,512},{768,640},{896,768... | collective-permute-start | bytes 786440 | tf_op jit(solution)/shard_map/ppermute | solution.py:22
  612.3 28.8 %collective-permute-start.8 = (f32[16,2,2,8,128]{4,3,2,0,1:T(8,128)}, f32[16,2,2,8,128]{4,3,2,0,1:T(8,128)S(1)}, u32[]{:S(2)}, u32[]{:S(2)}) collective-permute-start(f32[16,2,2,8,128]{4,3,2,0,1:T(8,128)} %get-tuple-element.529), channel_id=1, source_target_pairs={{0,128},{128,256},{256,384},{384,512},{512,640},{640,768},{768,896... | collective-permute-start | bytes 786440 | tf_op jit(solution)/shard_map/ppermute | solution.py:21
  620.0 8.6 %collective-permute-start.11 = (f32[16,2,2,256]{3,2,1,0:T(2,128)S(1)}, f32[16,2,2,256]{3,2,1,0:T(2,128)S(1)}, u32[]{:S(2)}, u32[]{:S(2)}) collective-permute-start(f32[16,2,2,256]{3,2,1,0:T(2,128)S(1)} %get-tuple-element.532), channel_id=1, source_target_pairs={{16,0},{32,16},{48,32},{64,48},{80,64},{96,80},{112,96},{0,112},{1... | collective-permute-start | bytes 196616 | tf_op jit(solution)/shard_map/ppermute | solution.py:22
  628.7 14.6 %copy-start.1 = (f32[3,8,32,128]{3,1,2,0:T(8,128)S(1)}, f32[3,8,32,128]{3,1,2,0:T(8,128)}, u32[]{:S(2)}) copy-start(f32[3,8,32,128]{3,1,2,0:T(8,128)} %copy.206) | copy-start | bytes 1179652
  628.7 14.6 %copy-start.3 = (f32[2,8,32,128]{3,1,0,2:T(8,128)S(1)}, f32[2,8,32,128]{3,1,0,2:T(8,128)}, u32[]{:S(2)}) copy-start(f32[2,8,32,128]{3,1,0,2:T(8,128)} %copy.205) | copy-start | bytes 786436
  628.7 14.6 %copy-start.4 = (f32[2,8,32,128]{3,1,0,2:T(8,128)S(1)}, f32[2,8,32,128]{3,1,0,2:T(8,128)}, u32[]{:S(2)}) copy-start(f32[2,8,32,128]{3,1,0,2:T(8,128)} %copy.207) | copy-start | bytes 786436
  628.7 14.6 %copy-start.8 = (f32[8,32,128]{2,0,1:T(8,128)S(1)}, f32[8,32,128]{2,0,1:T(8,128)}, u32[]{:S(2)}) copy-start(f32[8,32,128]{2,0,1:T(8,128)} %copy-done.7) | copy-start | bytes 393220
  (89 other events, 204.2 us)
where the time goes:
time: 717 us; the launch traced here: 705 us
  local copies, waits for them, and re-layouts  395 us (55%)
  other arithmetic  231 us (32%)
  starting transfers between devices  56 us (8%)
  waiting for transfers between devices  17.5 us (2%)
    another operation x166, local copies, waits for them, and re-layouts  101 us
    squeeze x224, local copies, waits for them, and re-layouts, outer_layers(): jnp.stack([face_layer(field, along, 0), face_layer(field, along, 1), face...  90 us
    dynamic_update_slice x64, other arithmetic, body(): lax.scan(stepper, conc, incoming, length=NT)  61.4 us
    add x48, other arithmetic, advance(): return field + (spread - carried + reaction)  39.9 us
    ppermute x6, starting transfers between devices, extended(): after = lax.ppermute(initial, axis, down)  38.9 us
    div x64, local copies, waits for them, and re-layouts, update(): (datum + face) / (1.0 + ROBIN)  35.5 us
    mul x64, local copies, waits for them, and re-layouts, advance(): speeds[0] * jnp.where(against[0], field - upper_z, field - lower_z)  32.7 us
    squeeze x32, other arithmetic, outer_layers(): jnp.stack([face_layer(field, along, 0), face_layer(field, along, 1), face...  31.7 us
  transfers between devices with their start and end apart: 12, of which 4 were waited for; matrix products, arithmetic and copies ran while one was open for 3% of the time, Pallas kernels for 0%

commit v1 on v0

v1 whole, which is shorter than its diff:
```python
import functools

import jax
import jax.numpy as jnp
from jax import lax
from jax.experimental import pallas as pl
from jax.experimental.pallas import tpu as pltpu
from jax.sharding import PartitionSpec as P

NT = 16
ROBIN = 0.5
DIFFUSE = 0.07
SHARE = 1.0 / (1.0 + ROBIN)

CZ, CX, CY = 8, 32, 128
XT = CX // 8
PAD = CX + 16
FIELD = 2 * CZ * PAD
AXES = ("gz", "gx", "gy")
Z0, Z1, X0, X1, Y0, Y1, SLOT = 0, 64, 128, 144, 160, 176, 192
SLOTS = 2 * (NT - 1)


def kernel(conc, speed, rates, region, flags, out, u, dense, raw, zone, az, ax, ay, cc, kk, send, recv, in_sem, out_sem, send_sem, recv_sem):
    def plane(row, tr, z):
        return row + (tr * CZ + z) * PAD + 8

    get_conc = pltpu.make_async_copy(conc, dense, in_sem.at[0])
    get_conc.start()
    get_speed = pltpu.make_async_copy(speed, raw.at[pl.ds(0, 3)], in_sem.at[1])
    get_rates = pltpu.make_async_copy(rates, raw.at[pl.ds(3, 2)], in_sem.at[2])
    get_region = pltpu.make_async_copy(region, zone, in_sem.at[3])
    get_speed.start()
    get_rates.start()
    get_region.start()

    near = []
    for name in AXES:
        n, me = lax.axis_size(name), lax.axis_index(name)
        near.append(({name: lax.rem(me + n - 1, n)}, {name: lax.rem(me + 1, n)}))
    barrier = pltpu.get_barrier_semaphore()
    for low, high in near:
        pl.semaphore_signal(barrier, inc=1, device_id=low, device_id_type=pl.DeviceIdType.MESH)
        pl.semaphore_signal(barrier, inc=1, device_id=high, device_id_type=pl.DeviceIdType.MESH)

    zero = jnp.zeros((8, CY), jnp.float32)
    for b in range(3):
        for tr in range(2):
            for z in range(CZ):
                u[pl.ds(plane(b * FIELD, tr, z) - 8, 8), :] = zero
                u[pl.ds(plane(b * FIELD, tr, z) + CX, 8), :] = zero

    lane = lax.broadcasted_iota(jnp.int32, (8, CY), 1)
    sub = lax.broadcasted_iota(jnp.int32, (8, CY), 0)
    first, last = lane == 0, lane == CY - 1
    group, place = lane // 4, lane % 4

    get_conc.wait()
    pl.semaphore_wait(barrier, 6)

    def copies(slot):
        result = []
        for src, dst, size, where in (
            (Z0, Z1, 64, near[0][0]),
            (Z1, Z0, 64, near[0][1]),
            (X0, X1, 16, near[1][0]),
            (X1, X0, 16, near[1][1]),
            (Y0, Y1, 16, near[2][0]),
            (Y0, Y0, 16, near[2][1]),
        ):
            result.append(
                pltpu.make_async_remote_copy(
                    send.at[slot, pl.ds(src, size), :],
                    recv.at[slot, pl.ds(dst, size), :],
                    send_sem,
                    recv_sem.at[slot],
                    device_id=where,
                    device_id_type=pl.DeviceIdType.MESH,
                )
            )
        return result

    def datum(inner, outer):
        return (inner - (1.0 - ROBIN) * outer) * SHARE

    def emit(slot, row, packed):
        moves = copies(slot)
        moves[0].start()
        moves[1].start()
        for tr in range(2):
            base = plane(row, tr, 0)

            def xrow(i):
                return u[pl.ds(base + i, CZ, stride=PAD), :]

            send[slot, pl.ds(X0 + 8 * tr, 8), :] = datum(xrow(1), xrow(0))
            send[slot, pl.ds(X1 + 8 * tr, 8), :] = datum(xrow(CX - 2), xrow(CX - 1))
            p = packed[tr]
            mixed = jnp.where(place == 0, datum(p, pltpu.roll(p, CY - 1, 1)), datum(p, pltpu.roll(p, 1, 1)))
            send[slot, pl.ds(Y0 + 8 * tr, 8), :] = mixed
        for m in moves[2:]:
            m.start()

    def gather_sends(slot, cells, packed, xt, z, field):
        for tr in range(2):
            if z == 1:
                send[slot, pl.ds(Z0 + CX * tr + 8 * xt, 8), :] = datum(field[tr, 1], field[tr, 0])
            if z == CZ - 1:
                send[slot, pl.ds(Z1 + CX * tr + 8 * xt, 8), :] = datum(field[tr, CZ - 2], field[tr, CZ - 1])
            k = z * XT + xt
            packed[tr] = jnp.where(group == k, pltpu.roll(cells[tr], (4 * k + 2) % CY, 1), packed[tr])

    packed = [zero, zero]
    for xt in range(XT):
        field = {}
        for z in range(CZ):
            cells = [dense[tr, z, pl.ds(8 * xt, 8), :] for tr in range(2)]
            for tr in range(2):
                u[pl.ds(plane(0, tr, z) + 8 * xt, 8), :] = cells[tr]
                field[tr, z] = cells[tr]
            gather_sends(0, cells, packed, xt, z, field)
    emit(0, 0, packed)

    get_speed.wait()
    get_rates.wait()
    get_region.wait()
    f = flags[0, 0, 0]
    against = [((f // (2**d)) % 2).astype(jnp.float32) for d in range(3)]
    for z in range(CZ):
        for xt in range(XT):
            at = pl.ds(z * CX + 8 * xt, 8)
            cell = pl.ds(8 * xt, 8)
            s = [raw[d, z, cell, :] for d in range(3)]
            low, high = [], []
            for d, ref in enumerate((az, ax, ay)):
                up = s[d] * against[d]
                low.append(DIFFUSE + (s[d] - up))
                high.append(DIFFUSE + up)
                ref[0, at, :] = low[d]
                ref[1, at, :] = high[d]
            own = jnp.where(first, low[2], 0.0) + jnp.where(last, high[2], 0.0)
            if z == 0:
                own = own + low[0]
            if z == CZ - 1:
                own = own + high[0]
            if xt == 0:
                own = own + jnp.where(sub == 0, low[1], 0.0)
            if xt == XT - 1:
                own = own + jnp.where(sub == 7, high[1], 0.0)
            centre = (1.0 - 6.0 * DIFFUSE) - ((s[0] + s[1]) + s[2])
            cc[0, at, :] = centre + own
            cc[1, at, :] = centre + own * SHARE
            react = zone[z, cell, :].astype(jnp.float32)
            kk[0, at, :] = react * raw[3, z, cell, :]
            kk[1, at, :] = react * raw[4, z, cell, :]

    def update(src, dst, slot, to_slot):
        which = 0 if slot is None else 1
        if slot is not None:
            mixed = []
            for tr in range(2):
                base = plane(src, tr, 0)
                u[pl.ds(base - 1, CZ, stride=PAD), :] = recv[slot, pl.ds(X0 + 8 * tr, 8), :]
                u[pl.ds(base + CX, CZ, stride=PAD), :] = recv[slot, pl.ds(X1 + 8 * tr, 8), :]
                from_low = recv[slot, pl.ds(Y0 + 8 * tr, 8), :]
                from_high = recv[slot, pl.ds(Y1 + 8 * tr, 8), :]
                mixed.append(jnp.where(place == 0, from_low, pltpu.roll(from_high, CY - 4, 1)))
        packed = [zero, zero]
        for xt in range(XT):
            now = {}
            field = {}
            for z in range(CZ):
                at = pl.ds(z * CX + 8 * xt, 8)
                k = z * XT + xt
                for tr in range(2):
                    for zz in (z, z + 1):
                        if zz < CZ and (tr, zz) not in now:
                            now[tr, zz] = u[pl.ds(plane(src, tr, zz) + 8 * xt, 8), :]
                coef = [az[0, at, :], az[1, at, :], ax[0, at, :], ax[1, at, :], ay[0, at, :], ay[1, at, :]]
                centre = cc[which, at, :]
                react = kk[1, at, :] * now[1, z] - kk[0, at, :] * now[0, z]
                cells = []
                for tr in range(2):
                    c = now[tr, z]
                    base = plane(src, tr, z) + 8 * xt
                    y_low = pltpu.roll(c, 1, 1)
                    y_high = pltpu.roll(c, CY - 1, 1)
                    if slot is None:
                        y_low = jnp.where(first, 0.0, y_low)
                        y_high = jnp.where(last, 0.0, y_high)
                    else:
                        ghost = pltpu.roll(mixed[tr], (CY - 4 * k) % CY, 1) if k else mixed[tr]
                        y_low = jnp.where(first, ghost, y_low)
                        y_high = jnp.where(last, ghost, y_high)
                    total = coef[4] * y_low + coef[5] * y_high
                    total = total + (coef[2] * u[pl.ds(base - 1, 8), :] + coef[3] * u[pl.ds(base + 1, 8), :])
                    z_low = now.get((tr, z - 1))
                    z_high = now.get((tr, z + 1))
                    if slot is not None:
                        if z == 0:
                            z_low = recv[slot, pl.ds(Z0 + CX * tr + 8 * xt, 8), :]
                        if z == CZ - 1:
                            z_high = recv[slot, pl.ds(Z1 + CX * tr + 8 * xt, 8), :]
                    if z_low is not None:
                        total = total + coef[0] * z_low
                    if z_high is not None:
                        total = total + coef[1] * z_high
                    total = total + centre * c
                    new = total + react if tr == 0 else total - react
                    u[pl.ds(plane(dst, tr, z) + 8 * xt, 8), :] = new
                    cells.append(new)
                    field[tr, z] = new
                if to_slot is not None:
                    gather_sends(to_slot, cells, packed, xt, z, field)
        if to_slot is not None:
            emit(to_slot, dst, packed)

    def rows(t):
        source = ((t + 15) // 16) * (1 + (t + 1) % 2)
        return pl.multiple_of(source * FIELD, 8), pl.multiple_of((1 + t % 2) * FIELD, 8)

    def wait_slot(slot):
        whole = recv.at[slot]
        pltpu.make_async_copy(whole, whole, recv_sem.at[slot]).wait()

    @pl.loop(0, NT - 2)
    def _(t):
        src, dst = rows(t)
        update(src, dst, None, t + 1)

    @pl.loop(0, NT - 1)
    def _(t):
        src, dst = rows(t)
        wait_slot(t)
        update(src, dst, t, NT - 1 + t)

    src, dst = rows(0)
    update(0, FIELD, 0, None)

    @pl.loop(1, NT)
    def _(t):
        src, dst = rows(t)
        wait_slot(NT - 2 + t)
        update(src, dst, NT - 2 + t, None)

    final = (1 + (NT - 1) % 2) * FIELD
    for tr in range(2):
        for z in range(CZ):
            dense[tr, z] = u[pl.ds(plane(final, tr, z), CX), :]
    put = pltpu.make_async_copy(dense, out, out_sem)
    put.start()
    pltpu.make_async_copy(send, send, send_sem).wait()
    put.wait()


def body(conc, speed, rates, region, flow_signs):
    hbm = pl.BlockSpec(memory_space=pltpu.HBM)
    f32 = jnp.float32
    return pl.pallas_call(
        kernel,
        out_shape=jax.ShapeDtypeStruct(conc.shape, f32),
        in_specs=[hbm, hbm, hbm, hbm, pl.BlockSpec(memory_space=pltpu.SMEM)],
        out_specs=hbm,
        scratch_shapes=[
            pltpu.VMEM((3 * FIELD, CY), f32),
            pltpu.VMEM((2, CZ, CX, CY), f32),
            pltpu.VMEM((5, CZ, CX, CY), f32),
            pltpu.VMEM((CZ, CX, CY), jnp.int32),
            pltpu.VMEM((2, CZ * CX, CY), f32),
            pltpu.VMEM((2, CZ * CX, CY), f32),
            pltpu.VMEM((2, CZ * CX, CY), f32),
            pltpu.VMEM((2, CZ * CX, CY), f32),
            pltpu.VMEM((2, CZ * CX, CY), f32),
            pltpu.VMEM((SLOTS, SLOT, CY), f32),
            pltpu.VMEM((SLOTS, SLOT, CY), f32),
            pltpu.SemaphoreType.DMA((4,)),
            pltpu.SemaphoreType.DMA,
            pltpu.SemaphoreType.DMA,
            pltpu.SemaphoreType.DMA((SLOTS,)),
        ],
        compiler_params=pltpu.CompilerParams(
            collective_id=0, has_side_effects=True, vmem_limit_bytes=32 * 1024 * 1024
        ),
    )(conc, speed, rates, region, flow_signs)


def solution(mesh):
    placed = (
        P(None, "gz", "gx", "gy"),
        P(None, "gz", "gx", "gy"),
        P(None, "gz", "gx", "gy"),
        P("gz", "gx", "gy"),
        P("gz", "gx", "gy"),
    )
    return jax.shard_map(
        body, mesh=mesh, in_specs=placed, out_specs=P(None, "gz", "gx", "gy"), check_vma=False
    )
```

time: 717 us -> 95 us (0.13)
  the two profiles are of different devices: /device:TPU:17 before, /device:TPU:14 now
where the time goes in v1:
time: 95 us; the launch traced here: 94.2 us
  Pallas kernels  89 us (94%)
  local copies, waits for them, and re-layouts  4.5 us (5%)
    pallas_call x1, Pallas kernels, body(): pl.pallas_call(kernel, out_shape=jax.ShapeDtypeStruct(conc.shape, f32), i...  89 us
    unnamed x9, local copies, waits for them, and re-layouts  4.5 us

profile of v1, /device:TPU:14, one launch (start us, length us, event | category | flops | bytes accessed | tf_op | source)
XLA Modules:
  0.0 94.2 jit_solution(12383874786806543669)
XLA Ops:
  0.7 0.0 copy-start
  0.7 1.0 %copy-done = f32[3,8,32,128]{3,2,1,0:T(8,128)S(1)} copy-done((f32[3,8,32,128]{3,2,1,0:T(8,128)S(1)}, f32[3,8,32,128]{3,2,1,0:T(8,128)}, u32[]{:S(2)}) %copy-start) | copy-done | bytes 393240
  1.6 0.0 copy-start.1
  1.7 0.9 %copy-done.1 = f32[2,8,32,128]{3,2,1,0:T(8,128)S(1)} copy-done((f32[2,8,32,128]{3,2,1,0:T(8,128)S(1)}, f32[2,8,32,128]{3,2,1,0:T(8,128)}, u32[]{:S(2)}) %copy-start.1) | copy-done | bytes 262168
  2.6 0.0 copy-start.2
  2.6 0.9 %copy-done.2 = f32[2,8,32,128]{3,2,1,0:T(8,128)S(1)} copy-done((f32[2,8,32,128]{3,2,1,0:T(8,128)S(1)}, f32[2,8,32,128]{3,2,1,0:T(8,128)}, u32[]{:S(2)}) %copy-start.2) | copy-done | bytes 262168
  3.5 0.0 copy-start.3
  3.6 0.9 copy-done.3
  4.5 89.0 %shard_map.55 = f32[2,8,32,128]{3,2,1,0:T(8,128)S(1)} custom-call(f32[2,8,32,128]{3,2,1,0:T(8,128)S(1)} %copy-done.1, f32[3,8,32,128]{3,2,1,0:T(8,128)S(1)} %copy-done, f32[2,8,32,128]{3,2,1,0:T(8,128)S(1)} %copy-done.2, s32[8,32,128]{2,1,0:T(8,128)S(1)} %copy-done.3, s32[1,1,1]{2,1,0:T(1,128)S(6)} %copy.7.flags), custom_call_target="tpu_custom_call" | custom-call | tf_op jit(solution)/shard_map/pallas_call | solution.py:259
  93.5 0.7 copy.8
Async XLA Ops:
  0.7 1.0 %copy-start = (f32[3,8,32,128]{3,2,1,0:T(8,128)S(1)}, f32[3,8,32,128]{3,2,1,0:T(8,128)}, u32[]{:S(2)}) copy-start(f32[3,8,32,128]{3,2,1,0:T(8,128)} %speed.1) | copy-start | bytes 1179652
  1.6 0.9 %copy-start.1 = (f32[2,8,32,128]{3,2,1,0:T(8,128)S(1)}, f32[2,8,32,128]{3,2,1,0:T(8,128)}, u32[]{:S(2)}) copy-start(f32[2,8,32,128]{3,2,1,0:T(8,128)} %conc.1) | copy-start | bytes 786436
  2.6 0.9 %copy-start.2 = (f32[2,8,32,128]{3,2,1,0:T(8,128)S(1)}, f32[2,8,32,128]{3,2,1,0:T(8,128)}, u32[]{:S(2)}) copy-start(f32[2,8,32,128]{3,2,1,0:T(8,128)} %rates.1) | copy-start | bytes 786436
  3.5 0.9 copy-start.3

commit v2 on v1

--- a/solution.py
+++ b/solution.py
@@ -21,9 +21,9 @@
 SLOTS = 2 * (NT - 1)
 
 
-def kernel(conc, speed, rates, region, flags, out, u, dense, raw, zone, az, ax, ay, cc, kk, send, recv, in_sem, out_sem, send_sem, recv_sem):
-    def plane(row, tr, z):
-        return row + (tr * CZ + z) * PAD + 8
+def kernel(conc, speed, rates, region, flags, out, ua, ub, dense, raw, zone, az, ax, ay, cc, kk, send, recv, in_sem, out_sem, send_sem, recv_sem):
+    def plane(tr, z):
+        return (tr * CZ + z) * PAD + 8
 
     get_conc = pltpu.make_async_copy(conc, dense, in_sem.at[0])
     get_conc.start()
@@ -44,11 +44,11 @@
         pl.semaphore_signal(barrier, inc=1, device_id=high, device_id_type=pl.DeviceIdType.MESH)
 
     zero = jnp.zeros((8, CY), jnp.float32)
-    for b in range(3):
+    for u in (ua, ub):
         for tr in range(2):
             for z in range(CZ):
-                u[pl.ds(plane(b * FIELD, tr, z) - 8, 8), :] = zero
-                u[pl.ds(plane(b * FIELD, tr, z) + CX, 8), :] = zero
+                u[pl.ds(plane(tr, z) - 8, 8), :] = zero
+                u[pl.ds(plane(tr, z) + CX, 8), :] = zero
 
     lane = lax.broadcasted_iota(jnp.int32, (8, CY), 1)
     sub = lax.broadcasted_iota(jnp.int32, (8, CY), 0)
@@ -83,12 +83,12 @@
     def datum(inner, outer):
         return (inner - (1.0 - ROBIN) * outer) * SHARE
 
-    def emit(slot, row, packed):
+    def emit(slot, u, packed):
         moves = copies(slot)
         moves[0].start()
         moves[1].start()
         for tr in range(2):
-            base = plane(row, tr, 0)
+            base = plane(tr, 0)
 
             def xrow(i):
                 return u[pl.ds(base + i, CZ, stride=PAD), :]
@@ -116,10 +116,10 @@
         for z in range(CZ):
             cells = [dense[tr, z, pl.ds(8 * xt, 8), :] for tr in range(2)]
             for tr in range(2):
-                u[pl.ds(plane(0, tr, z) + 8 * xt, 8), :] = cells[tr]
+                ua[pl.ds(plane(tr, z) + 8 * xt, 8), :] = cells[tr]
                 field[tr, z] = cells[tr]
             gather_sends(0, cells, packed, xt, z, field)
-    emit(0, 0, packed)
+    emit(0, ua, packed)
 
     get_speed.wait()
     get_rates.wait()
@@ -159,9 +159,9 @@
         if slot is not None:
             mixed = []
             for tr in range(2):
-                base = plane(src, tr, 0)
-                u[pl.ds(base - 1, CZ, stride=PAD), :] = recv[slot, pl.ds(X0 + 8 * tr, 8), :]
-                u[pl.ds(base + CX, CZ, stride=PAD), :] = recv[slot, pl.ds(X1 + 8 * tr, 8), :]
+                base = plane(tr, 0)
+                src[pl.ds(base - 1, CZ, stride=PAD), :] = recv[slot, pl.ds(X0 + 8 * tr, 8), :]
+                src[pl.ds(base + CX, CZ, stride=PAD), :] = recv[slot, pl.ds(X1 + 8 * tr, 8), :]
                 from_low = recv[slot, pl.ds(Y0 + 8 * tr, 8), :]
                 from_high = recv[slot, pl.ds(Y1 + 8 * tr, 8), :]
                 mixed.append(jnp.where(place == 0, from_low, pltpu.roll(from_high, CY - 4, 1)))
@@ -175,14 +175,14 @@
                 for tr in range(2):
                     for zz in (z, z + 1):
                         if zz < CZ and (tr, zz) not in now:
-                            now[tr, zz] = u[pl.ds(plane(src, tr, zz) + 8 * xt, 8), :]
+                            now[tr, zz] = src[pl.ds(plane(tr, zz) + 8 * xt, 8), :]
                 coef = [az[0, at, :], az[1, at, :], ax[0, at, :], ax[1, at, :], ay[0, at, :], ay[1, at, :]]
                 centre = cc[which, at, :]
                 react = kk[1, at, :] * now[1, z] - kk[0, at, :] * now[0, z]
                 cells = []
                 for tr in range(2):
                     c = now[tr, z]
-                    base = plane(src, tr, z) + 8 * xt
+                    base = plane(tr, z) + 8 * xt
                     y_low = pltpu.roll(c, 1, 1)
                     y_high = pltpu.roll(c, CY - 1, 1)
                     if slot is None:
@@ -193,7 +193,7 @@
                         y_low = jnp.where(first, ghost, y_low)
                         y_high = jnp.where(last, ghost, y_high)
                     total = coef[4] * y_low + coef[5] * y_high
-                    total = total + (coef[2] * u[pl.ds(base - 1, 8), :] + coef[3] * u[pl.ds(base + 1, 8), :])
+                    total = total + (coef[2] * src[pl.ds(base - 1, 8), :] + coef[3] * src[pl.ds(base + 1, 8), :])
                     z_low = now.get((tr, z - 1))
                     z_high = now.get((tr, z + 1))
                     if slot is not None:
@@ -207,7 +207,7 @@
                         total = total + coef[1] * z_high
                     total = total + centre * c
                     new = total + react if tr == 0 else total - react
-                    u[pl.ds(plane(dst, tr, z) + 8 * xt, 8), :] = new
+                    dst[pl.ds(base, 8), :] = new
                     cells.append(new)
                     field[tr, z] = new
                 if to_slot is not None:
@@ -215,9 +215,16 @@
         if to_slot is not None:
             emit(to_slot, dst, packed)
 
-    def rows(t):
-        source = ((t + 15) // 16) * (1 + (t + 1) % 2)
-        return pl.multiple_of(source * FIELD, 8), pl.multiple_of((1 + t % 2) * FIELD, 8)
+    def step(slot, to_slot):
+        update(ua, ub, slot, to_slot)
+        for tr in range(2):
+            for z in range(CZ):
+                ua[pl.ds(plane(tr, z), CX), :] = ub[pl.ds(plane(tr, z), CX), :]
+
+    def restart():
+        for tr in range(2):
+            for z in range(CZ):
+                ua[pl.ds(plane(tr, z), CX), :] = dense[tr, z]
 
     def wait_slot(slot):
         whole = recv.at[slot]
@@ -225,28 +232,28 @@
 
     @pl.loop(0, NT - 2)
     def _(t):
-        src, dst = rows(t)
-        update(src, dst, None, t + 1)
+        step(None, t + 1)
+
+    restart()
 
     @pl.loop(0, NT - 1)
     def _(t):
-        src, dst = rows(t)
         wait_slot(t)
-        update(src, dst, t, NT - 1 + t)
-
-    src, dst = rows(0)
-    update(0, FIELD, 0, None)
-
-    @pl.loop(1, NT)
+        step(t, NT - 1 + t)
+
+    restart()
+
+    @pl.loop(0, NT)
     def _(t):
-        src, dst = rows(t)
-        wait_slot(NT - 2 + t)
-        update(src, dst, NT - 2 + t, None)
-
-    final = (1 + (NT - 1) % 2) * FIELD
+        @pl.when(t > 0)
+        def _():
+            wait_slot(NT - 2 + t)
+
+        step(((t + NT - 1) // NT) * (NT - 2 + t), None)
+
     for tr in range(2):
         for z in range(CZ):
-            dense[tr, z] = u[pl.ds(plane(final, tr, z), CX), :]
+            dense[tr, z] = ua[pl.ds(plane(tr, z), CX), :]
     put = pltpu.make_async_copy(dense, out, out_sem)
     put.start()
     pltpu.make_async_copy(send, send, send_sem).wait()
@@ -262,7 +269,8 @@
         in_specs=[hbm, hbm, hbm, hbm, pl.BlockSpec(memory_space=pltpu.SMEM)],
         out_specs=hbm,
         scratch_shapes=[
-            pltpu.VMEM((3 * FIELD, CY), f32),
+            pltpu.VMEM((FIELD, CY), f32),
+            pltpu.VMEM((FIELD, CY), f32),
             pltpu.VMEM((2, CZ, CX, CY), f32),
             pltpu.VMEM((5, CZ, CX, CY), f32),
             pltpu.VMEM((CZ, CX, CY), jnp.int32),
@@ -279,7 +287,7 @@
             pltpu.SemaphoreType.DMA((SLOTS,)),
         ],
         compiler_params=pltpu.CompilerParams(
-            collective_id=0, has_side_effects=True, vmem_limit_bytes=32 * 1024 * 1024
+            collective_id=0, has_side_effects=True, vmem_limit_bytes=60 * 1024 * 1024
         ),
     )(conc, speed, rates, region, flow_signs)
 

time: 95 us -> 56.9 us (0.60)
  Pallas kernels: 89 us -> 54.4 us
  local copies, waits for them, and re-layouts: 4.5 us -> 1.67 us
    pallas_call x1, Pallas kernels: 89 us -> 54.4 us  [body(): pl.pallas_call(kernel, out_shape=jax.ShapeDtypeStruct(conc.shape, f32), i...]
    unnamed x9 -> x1, local copies, waits for them, and re-layouts: 4.5 us -> 1.67 us
where the time goes in v2:
time: 56.9 us; the launch traced here: 56.7 us
  Pallas kernels  54.4 us (96%)
  local copies, waits for them, and re-layouts  1.67 us (3%)
  between operations  0.66 us (1%)
    pallas_call x1, Pallas kernels, body(): pl.pallas_call(kernel, out_shape=jax.ShapeDtypeStruct(conc.shape, f32), i...  54.4 us
    unnamed x1, local copies, waits for them, and re-layouts  1.67 us

profile of v2, /device:TPU:14, one launch (start us, length us, event | category | flops | bytes accessed | tf_op | source)
XLA Modules:
  0.0 56.7 jit_solution(10856695456821417854)
XLA Ops:
  0.7 54.4 %shard_map.55 = f32[2,8,32,128]{3,2,1,0:T(8,128)} custom-call(f32[2,8,32,128]{3,2,1,0:T(8,128)} %conc.1, f32[3,8,32,128]{3,2,1,0:T(8,128)} %speed.1, f32[2,8,32,128]{3,2,1,0:T(8,128)} %rates.1, s32[8,32,128]{2,1,0:T(8,128)} %region.1, s32[1,1,1]{2,1,0:T(1,128)S(6)} %copy.7.flags), custom_call_target="tpu_custom_call" | custom-call | tf_op jit(solution)/shard_map/pallas_call | solution.py:266
  55.1 1.7 %copy.8 = f32[2,8,32,128]{3,2,1,0:T(8,128)} copy(f32[2,8,32,128]{3,2,1,0:T(8,128)} %shard_map.55) | data formatting | bytes 524288
